TPU v7x, 32 devices: a whole 2x2x4 slice. The times are simulated.
32 devices in a mesh: gx: 8 (over y, x, core), gy: 4 (over z).
Axes of the slice: x: 2, y: 2, z: 4, core: 2. Of those that a mesh axis runs over, the one named last changes fastest.
Arguments:
- test_block: float32 [32, 8, 128, 512], P(None, None, 'gx', 'gy'), may hold values from -1500 to 1500, as said below
- kappa_sq: float32 [8, 128, 512], P(None, 'gx', 'gy'), may hold values from 0.05 to 2
Outputs:
- basis: float32 [32, 8, 128, 512], P(None, None, 'gx', 'gy')
Inputs may be any that keep to these rules, and one draw needn't show every extreme that they name: `test_block`: real-valued entries.
All inputs are finite; a program needn't handle non-finite values.
Results may differ from a plain program's by a relative error of at most 0.0003.
Values sent between devices are 32-bit elements; how exact they have to be, the bound alone decides.
A program may use at most 64 MiB of HBM per device.

v0:
```python
import math

import jax
import jax.numpy as jnp
from jax import lax
from jax.sharding import PartitionSpec as P


def extended(block, sides, width):
    for axis, dim in sides:
        count = lax.axis_size(axis)
        forward = [(i, i + 1) for i in range(count - 1)]
        backward = [(target, source) for source, target in forward]
        low = lax.ppermute(
            lax.slice_in_dim(block, block.shape[dim] - width, None, axis=dim), axis, forward
        )
        high = lax.ppermute(lax.slice_in_dim(block, 0, width, axis=dim), axis, backward)
        block = jnp.concatenate([low, block, high], axis=dim)
    return block


def stencil(padded, coefficient):
    center = padded[:, :, 1:-1, 1:-1]
    neighbours = padded[:, :, 2:, 1:-1] + padded[:, :, :-2, 1:-1]
    neighbours = neighbours + padded[:, :, 1:-1, 2:] + padded[:, :, 1:-1, :-2]
    z_padded = jnp.pad(center, ((0, 0), (1, 1), (0, 0), (0, 0)))
    neighbours = neighbours + z_padded[:, 2:] + z_padded[:, :-2]
    return (6.0 + coefficient) * center - neighbours


def lower_solve(factor, block):
    return lax.linalg.triangular_solve(factor, block, left_side=True, lower=True)


def merge_factors(stacked):
    summed = jnp.einsum("nij,nkj->ik", stacked, stacked, precision=lax.Precision.HIGHEST)
    return jnp.linalg.cholesky(summed)


def merged_factor(gram_matrix):
    stacked = lax.all_gather(gram_matrix[None], "gx", axis=0, tiled=True)
    column_factor = jnp.linalg.cholesky(jnp.sum(stacked, axis=0))
    stacked_columns = lax.all_gather(column_factor[None], "gy", axis=0, tiled=True)
    return merge_factors(stacked_columns)


def body(test_block, kappa_sq):
    cols_here, depth_here, x_cells, y_cells = test_block.shape
    widened = extended(test_block, (("gx", 2), ("gy", 3)), 2)
    coefficient_wide = extended(kappa_sq, (("gx", 1), ("gy", 2)), 1)
    first_pass = stencil(widened, coefficient_wide)
    x_index = lax.axis_index("gx") * x_cells - 1 + jnp.arange(x_cells + 2, dtype=jnp.int32)
    y_index = lax.axis_index("gy") * y_cells - 1 + jnp.arange(y_cells + 2, dtype=jnp.int32)
    x_inside = (x_index >= 0) & (x_index < x_cells * lax.axis_size("gx"))
    y_inside = (y_index >= 0) & (y_index < y_cells * lax.axis_size("gy"))
    inside_mask = x_inside[:, None] & y_inside[None, :]
    first_pass = jnp.where(inside_mask[None, None], first_pass, 0.0)
    sample = stencil(first_pass, kappa_sq)
    flattened = sample.reshape(cols_here, -1)
    gram_one = jnp.dot(flattened, flattened.T, precision=lax.Precision.HIGHEST)
    factor_one = merged_factor(gram_one)
    partial_value = lower_solve(factor_one, flattened)
    gram_two = jnp.dot(partial_value, partial_value.T, precision=lax.Precision.HIGHEST)
    factor_two = merged_factor(gram_two)
    scale_factor = math.sqrt(flattened.shape[1] * lax.axis_size("gx") * lax.axis_size("gy"))
    result = lower_solve(factor_two, partial_value) * scale_factor
    return result.reshape(cols_here, depth_here, x_cells, y_cells)


def solution(mesh):
    in_specs = (P(None, None, "gx", "gy"), P(None, "gx", "gy"))
    out_specs = P(None, None, "gx", "gy")
    return jax.shard_map(body, mesh=mesh, in_specs=in_specs, out_specs=out_specs, check_vma=False)
```

profile of v0, /device:TPU:0, one launch (start us, length us, event | category | flops | bytes accessed | tf_op | source)
XLA Modules:
  0.0 161.8 jit_solution(3179271641019895300)
XLA Ops:
  2.0 2.4 %collective-permute-start.4 = (f32[32,8,2,128]{3,1,2,0:T(8,128)S(1)}, f32[32,8,2,128]{3,1,2,0:T(8,128)S(1)}, u32[]{:S(2)}, u32[]{:S(2)}) collective-permute-start(f32[32,8,2,128]{3,1,2,0:T(8,128)S(1)} %copy.99), channel_id=1, source_target_pairs={{0,4},{4,8},{8,12},{12,16},{16,20},{20,24},{24,28},{1,5},{5,9},{9,... | collective-permute-start | bytes 786440 | tf_op jit(solution)/shard_map/ppermute | solution.py:14
  6.4 5.1 %collective-permute-start = (f32[8,1,128]{2,0,1:T(8,128)S(1)}, f32[8,1,128]{2,0,1:T(8,128)S(1)}, u32[]{:S(2)}, u32[]{:S(2)}) collective-permute-start(f32[8,1,128]{2,0,1:T(8,128)S(1)} %copy.112), channel_id=1, source_target_pairs={{0,4},{4,8},{8,12},{12,16},{16,20},{20,24},{24,28},{1,5},{5,9},{9,... | collective-permute-start | bytes 12296 | tf_op jit(solution)/shard_map/ppermute | solution.py:14
  13.9 4.7 %copy.82 = f32[32,8,16,128]{0,1,3,2:T(8,128)} copy(f32[32,8,16,128]{3,2,1,0:T(8,128)S(1)} %copy-done.1) | data formatting | bytes 4194304 | tf_op args[0]
  19.3 3.5 %collective-permute-start.2 = (f32[8,18,1]{2,0,1:T(8,128)}, f32[8,18,1]{2,0,1:T(8,128)S(1)}, u32[]{:S(2)}, u32[]{:S(2)}) collective-permute-start(f32[8,18,1]{2,0,1:T(8,128)} %get-tuple-element.11), channel_id=1, source_target_pairs={{0,1},{1,2},{2,3},{4,5},{5,6},{6,7},{8,9},{9,10},{10,11},{12,13},{... | collective-permute-start | bytes 1736 | tf_op jit(solution)/shard_map/ppermute | solution.py:14
  25.0 8.4 %pad_maximum_fusion = f32[32,8,20,128]{0,1,3,2:T(8,128)} fusion(f32[32,8,2,128]{0,1,3,2:T(8,128)S(1)} %copy.83, f32[32,8,16,128]{0,1,3,2:T(8,128)} %copy.82, f32[32,8,2,128]{0,1,3,2:T(8,128)S(1)} %copy.81), kind=kLoop, calls=%fused_computation.3 | loop fusion | flops 1310720 | bytes 5242880 | tf_op jit(solution)/shard_map/concatenate | solution.py:18
  34.4 4.6 %collective-permute-start.6 = (f32[32,8,20,2]{0,1,3,2:T(8,128)S(1)}, f32[32,8,20,2]{0,1,3,2:T(8,128)S(1)}, u32[]{:S(2)}, u32[]{:S(2)}) collective-permute-start(f32[32,8,20,2]{0,1,3,2:T(8,128)S(1)} %get-tuple-element.6), channel_id=1, source_target_pairs={{0,1},{1,2},{2,3},{4,5},{5,6},{6,7},{8,9},{9,10},{10,11},{12,13},{... | collective-permute-start | bytes 122888 | tf_op jit(solution)/shard_map/ppermute | solution.py:14
  41.5 8.4 %copy.85 = f32[32,8,20,128]{3,1,2,0:T(8,128)} copy(f32[32,8,20,128]{0,1,3,2:T(8,128)} %pad_maximum_fusion) | data formatting | bytes 5242880 | tf_op jit(solution)/shard_map/concatenate | solution.py:18
  49.9 2.2 %copy.84 = f32[32,8,20,2]{3,1,2,0:T(8,128)S(1)} copy(f32[32,8,20,2]{0,1,3,2:T(8,128)S(1)} %collective-permute-done.6) | data formatting | bytes 81920 | tf_op jit(solution)/shard_map/ppermute | solution.py:14
  52.1 3.5 %copy.86 = f32[32,8,20,2]{3,1,2,0:T(8,128)} copy(f32[32,8,20,2]{0,1,3,2:T(8,128)S(1)} %collective-permute-done.7) | data formatting | bytes 81920 | tf_op jit(solution)/shard_map/ppermute | solution.py:17
  55.6 4.6 %pad_maximum_fusion.1 = f32[32,8,20,132]{3,1,2,0:T(8,128)S(1)} fusion(f32[32,8,20,2]{3,1,2,0:T(8,128)} %copy.86, f32[32,8,20,128]{3,1,2,0:T(8,128)} %copy.85, f32[32,8,20,2]{3,1,2,0:T(8,128)S(1)} %copy.84), kind=kLoop, calls=%fused_computation.4 | loop fusion | flops 1351680 | bytes 5406720 | tf_op jit(solution)/shard_map/concatenate | solution.py:18
  60.3 3.4 %slice.102 = f32[32,8,18,130]{3,1,2,0:T(8,128)} slice(f32[32,8,20,132]{3,1,2,0:T(8,128)S(1)} %pad_maximum_fusion.1), slice={[0:32], [0:8], [1:19], [1:131]} | slice | bytes 4792320 | tf_op jit(solution)/shard_map/slice | solution.py:23
  63.7 9.1 %fusion.3 = f32[32,8,18,130]{3,1,2,0:T(8,128)S(1)} fusion(f32[32,8,18,130]{3,1,2,0:T(8,128)} %slice.102, f32[32,8,20,128]{3,1,2,0:T(8,128)} %copy.85, f32[32,8,20,2]{3,1,2,0:T(8,128)S(1)} %copy.84, f32[32,8,20,2]{3,1,2,0:T(8,128)S(1)} %copy-done, f32[32,8,20,132]{3,1,2,0:T(8,128)S(1)} %pad_maximum_fusion.1, f32[8,18,130]{2,0,1:T(8,128)S(1)} %maximum_add_fusion, ...), kind=kLoop, calls=%fused_computation.10 | loop fusion | flops 5990400 | bytes 12365220 | tf_op jit(solution)/shard_map/jit(_where)/select_n | solution.py:57
  75.1 2.8 %fusion.15 = f32[32,32]{1,0:T(8,128)S(1)} fusion(f32[32,8,16,128]{3,1,2,0:T(8,128)S(1)} %fusion.8), kind=kOutput, calls=%fused_computation.28 | convolution fusion | flops 201326592 | bytes 2101248 | tf_op jit(solution)/shard_map/dot_general | solution.py:60
  79.6 13.5 %all-gather = f32[256,32]{1,0:T(8,128)S(1)} all-gather(f32[32,32]{1,0:T(8,128)S(1)} %fusion.15), channel_id=2, replica_groups=mesh['gx'=8,'gy'=4] {'gx'}, dimensions={0}, use_global_device_ids=true | all-gather | bytes 36864 | tf_op jit(solution)/shard_map/all_gather | solution.py:41
  93.2 2.9 %cholesky.74 = f32[32,32]{1,0:T(8,128)S(1)} custom-call(f32[32,32]{1,0:T(8,128)S(1)} %fusion.25), custom_call_target="Cholesky" | custom-call | tf_op jit(solution)/shard_map/jit(cholesky)/cholesky | solution.py:42
  97.6 14.9 %all-gather.1 = f32[128,32]{1,0:T(8,128)S(1)} all-gather(f32[32,32]{1,0:T(8,128)S(1)} %fusion.27), channel_id=3, replica_groups=mesh['gx'=8,'gy'=4] {'gy'}, dimensions={0}, use_global_device_ids=true | all-gather | bytes 20480 | tf_op jit(solution)/shard_map/all_gather | solution.py:43
  112.7 2.9 %cholesky.85 = f32[32,32]{1,0:T(8,128)S(1)} custom-call(f32[32,32]{1,0:T(8,128)S(1)} %fusion.24), custom_call_target="Cholesky" | custom-call | tf_op jit(solution)/shard_map/jit(cholesky)/cholesky | solution.py:37
  117.1 2.4 %custom-call.6 = f32[1,32,32]{1,2,0:T(8,128)S(1)} custom-call(f32[1,32,32]{2,1,0:T(8,128)S(1)} %fusion.18), custom_call_target="InvertDiagBlocksLowerTriangular" | custom-call | tf_op jit(solution)/shard_map/triangular_solve/custom-call.0 | solution.py:32
  119.6 4.6 %fusion.9 = f32[32,16384]{1,0:T(8,128)S(1)} fusion(f32[4,8,128,128]{3,2,1,0:T(8,128)} %bitcast.54, f32[1,32,32]{1,2,0:T(8,128)S(1)} %custom-call.6), kind=kOutput, calls=%fused_computation.19 | convolution fusion | flops 201326592 | bytes 4198400 | tf_op jit(solution)/shard_map/triangular_solve/dot.1 | solution.py:32
  125.9 7.8 %all-gather.2 = f32[256,32]{1,0:T(8,128)S(1)} all-gather(f32[32,32]{1,0:T(8,128)S(1)} %fusion.38), channel_id=4, replica_groups=mesh['gx'=8,'gy'=4] {'gx'}, dimensions={0}, use_global_device_ids=true | all-gather | bytes 36864 | tf_op jit(solution)/shard_map/all_gather | solution.py:41
  133.8 2.9 %cholesky.96 = f32[32,32]{1,0:T(8,128)S(1)} custom-call(f32[32,32]{1,0:T(8,128)S(1)} %fusion.22), custom_call_target="Cholesky" | custom-call | tf_op jit(solution)/shard_map/jit(cholesky)/cholesky | solution.py:42
  138.0 13.2 %all-gather.3 = f32[128,32]{1,0:T(8,128)S(1)} all-gather(f32[32,32]{1,0:T(8,128)S(1)} %fusion.26), channel_id=5, replica_groups=mesh['gx'=8,'gy'=4] {'gy'}, dimensions={0}, use_global_device_ids=true | all-gather | bytes 20480 | tf_op jit(solution)/shard_map/all_gather | solution.py:43
  151.5 2.9 %cholesky.107 = f32[32,32]{1,0:T(8,128)S(1)} custom-call(f32[32,32]{1,0:T(8,128)S(1)} %fusion.21), custom_call_target="Cholesky" | custom-call | tf_op jit(solution)/shard_map/jit(cholesky)/cholesky | solution.py:37
  155.8 2.4 %custom-call.7 = f32[1,32,32]{1,2,0:T(8,128)S(1)} custom-call(f32[1,32,32]{2,1,0:T(8,128)S(1)} %fusion.19), custom_call_target="InvertDiagBlocksLowerTriangular" | custom-call | tf_op jit(solution)/shard_map/triangular_solve/custom-call.0 | solution.py:32
  (67 shorter events, 28.4 us)
Async XLA Ops:
  0.0 13.8 %copy-start.1 = (f32[32,8,16,128]{3,2,1,0:T(8,128)S(1)}, f32[32,8,16,128]{3,2,1,0:T(8,128)}, u32[]{:S(2)}) copy-start(f32[32,8,16,128]{3,2,1,0:T(8,128)} %param.5) | copy-start | bytes 6291460
  2.0 22.2 %collective-permute-start.4 = (f32[32,8,2,128]{3,1,2,0:T(8,128)S(1)}, f32[32,8,2,128]{3,1,2,0:T(8,128)S(1)}, u32[]{:S(2)}, u32[]{:S(2)}) collective-permute-start(f32[32,8,2,128]{3,1,2,0:T(8,128)S(1)} %copy.99), channel_id=1, source_target_pairs={{0,4},{4,8},{8,12},{12,16},{16,20},{20,24},{24,28},{1,5},{5,9},{9,... | collective-permute-start | bytes 786440 | tf_op jit(solution)/shard_map/ppermute | solution.py:14
  4.4 20.2 %collective-permute-start.5 = (f32[32,8,2,128]{3,1,2,0:T(8,128)S(1)}, f32[32,8,2,128]{3,1,2,0:T(8,128)S(1)}, u32[]{:S(2)}, u32[]{:S(2)}) collective-permute-start(f32[32,8,2,128]{3,1,2,0:T(8,128)S(1)} %copy.100), channel_id=1, source_target_pairs={{4,0},{8,4},{12,8},{16,12},{20,16},{24,20},{28,24},{5,1},{9,5},{13... | collective-permute-start | bytes 786440 | tf_op jit(solution)/shard_map/ppermute | solution.py:17
  6.4 12.1 %collective-permute-start = (f32[8,1,128]{2,0,1:T(8,128)S(1)}, f32[8,1,128]{2,0,1:T(8,128)S(1)}, u32[]{:S(2)}, u32[]{:S(2)}) collective-permute-start(f32[8,1,128]{2,0,1:T(8,128)S(1)} %copy.112), channel_id=1, source_target_pairs={{0,4},{4,8},{8,12},{12,16},{16,20},{20,24},{24,28},{1,5},{5,9},{9,... | collective-permute-start | bytes 12296 | tf_op jit(solution)/shard_map/ppermute | solution.py:14
  11.6 7.0 %collective-permute-start.1 = (f32[8,1,128]{2,0,1:T(8,128)S(1)}, f32[8,1,128]{2,0,1:T(8,128)S(1)}, u32[]{:S(2)}, u32[]{:S(2)}) collective-permute-start(f32[8,1,128]{2,0,1:T(8,128)S(1)} %copy.113), channel_id=1, source_target_pairs={{4,0},{8,4},{12,8},{16,12},{20,16},{24,20},{28,24},{5,1},{9,5},{13... | collective-permute-start | bytes 12296 | tf_op jit(solution)/shard_map/ppermute | solution.py:17
  13.8 4.7 %copy-start.2 = (f32[8,16,128]{2,1,0:T(8,128)S(1)}, f32[8,16,128]{2,1,0:T(8,128)}, u32[]{:S(2)}) copy-start(f32[8,16,128]{2,1,0:T(8,128)} %param.6) | copy-start | bytes 196612
  19.3 21.1 %collective-permute-start.2 = (f32[8,18,1]{2,0,1:T(8,128)}, f32[8,18,1]{2,0,1:T(8,128)S(1)}, u32[]{:S(2)}, u32[]{:S(2)}) collective-permute-start(f32[8,18,1]{2,0,1:T(8,128)} %get-tuple-element.11), channel_id=1, source_target_pairs={{0,1},{1,2},{2,3},{4,5},{5,6},{6,7},{8,9},{9,10},{10,11},{12,13},{... | collective-permute-start | bytes 1736 | tf_op jit(solution)/shard_map/ppermute | solution.py:14
  22.8 17.7 %collective-permute-start.3 = (f32[8,18,1]{2,0,1:T(8,128)S(1)}, f32[8,18,1]{2,0,1:T(8,128)}, u32[]{:S(2)}, u32[]{:S(2)}) collective-permute-start(f32[8,18,1]{2,0,1:T(8,128)S(1)} %get-tuple-element.12), channel_id=1, source_target_pairs={{1,0},{2,1},{3,2},{5,4},{6,5},{7,6},{9,8},{10,9},{11,10},{13,12},{... | collective-permute-start | bytes 1736 | tf_op jit(solution)/shard_map/ppermute | solution.py:17
  34.4 15.5 %collective-permute-start.6 = (f32[32,8,20,2]{0,1,3,2:T(8,128)S(1)}, f32[32,8,20,2]{0,1,3,2:T(8,128)S(1)}, u32[]{:S(2)}, u32[]{:S(2)}) collective-permute-start(f32[32,8,20,2]{0,1,3,2:T(8,128)S(1)} %get-tuple-element.6), channel_id=1, source_target_pairs={{0,1},{1,2},{2,3},{4,5},{5,6},{6,7},{8,9},{9,10},{10,11},{12,13},{... | collective-permute-start | bytes 122888 | tf_op jit(solution)/shard_map/ppermute | solution.py:14
  39.0 13.2 %collective-permute-start.7 = (f32[32,8,20,2]{0,1,3,2:T(8,128)S(1)}, f32[32,8,20,2]{0,1,3,2:T(8,128)S(1)}, u32[]{:S(2)}, u32[]{:S(2)}) collective-permute-start(f32[32,8,20,2]{0,1,3,2:T(8,128)S(1)} %get-tuple-element.8), channel_id=1, source_target_pairs={{1,0},{2,1},{3,2},{5,4},{6,5},{7,6},{9,8},{10,9},{11,10},{13,12},{... | collective-permute-start | bytes 122888 | tf_op jit(solution)/shard_map/ppermute | solution.py:17
  60.3 3.4 %copy-start = (f32[32,8,20,2]{3,1,2,0:T(8,128)S(1)}, f32[32,8,20,2]{3,1,2,0:T(8,128)}, u32[]{:S(2)}) copy-start(f32[32,8,20,2]{3,1,2,0:T(8,128)} %copy.86) | copy-start | bytes 122884
where the time goes:
time: 163 us; the launch traced here: 162 us
  blocking collectives  49.4 us (30%)
  other arithmetic  47.9 us (29%)
  local copies, waits for them, and re-layouts  31.8 us (20%)
  starting transfers between devices  20.9 us (13%)
  matrix products  11.5 us (7%)
    all_gather x2, blocking collectives, merged_factor(): lax.all_gather(column_factor[None], 'gy', axis=0, tiled=True)  28.1 us
    all_gather x2, blocking collectives, merged_factor(): stacked = lax.all_gather(gram_matrix[None], 'gx', axis=0, tiled=True)  21.3 us
    ppermute x4, starting transfers between devices, extended(): lax.ppermute(lax.slice_in_dim(block, block.shape[dim] - width, None, axis...  15.5 us
    concatenate x2, other arithmetic, extended(): block = jnp.concatenate([low, block, high], axis=dim)  13 us
    select_n x1, other arithmetic, body(): first_pass = jnp.where(inside_mask[None, None], first_pass, 0.0)  9.07 us
    concatenate x2, local copies, waits for them, and re-layouts, extended(): block = jnp.concatenate([low, block, high], axis=dim)  8.4 us
    another operation x6, other arithmetic, merged_factor(): column_factor = jnp.linalg.cholesky(jnp.sum(stacked, axis=0))  7.27 us
    another operation x6, other arithmetic, merge_factors(): return jnp.linalg.cholesky(summed)  7.27 us
  transfers between devices with their start and end apart: 8, of which 0 were waited for; matrix products, arithmetic and copies ran while one was open for 18% of the time, Pallas kernels for 0%

commit v1 on v0

v1 whole, which is shorter than its diff:
```python
import functools
import math

import jax
import jax.numpy as jnp
from jax import lax
from jax.experimental import pallas as pl
from jax.experimental.pallas import tpu as pltpu
from jax.sharding import PartitionSpec as P

F32 = jnp.float32
BF16 = jnp.bfloat16
LANES = 128


def split(value, terms):
    pieces = []
    for _ in range(terms):
        piece = value.astype(BF16)
        pieces.append(piece)
        value = value - piece.astype(F32)
    return pieces


def fold_rows(block, cols, terms):
    total = block[:cols]
    for i in range(1, terms):
        total = total + block[i * cols:(i + 1) * cols]
    return total


def inverse_factor(gram, cols):
    rows = lax.broadcasted_iota(jnp.int32, (cols, 2 * cols), 0)
    lanes = lax.broadcasted_iota(jnp.int32, (cols, 2 * cols), 1)
    identity = jnp.where(rows + cols == lanes, 1.0, 0.0).astype(F32)
    work = jnp.concatenate([gram, identity[:, cols:]], axis=1)
    pivots = jnp.zeros((cols, 2 * cols), F32)
    for j in range(cols):
        column = jnp.broadcast_to(work[:, j:j + 1], (cols, 2 * cols))
        pivot = column[j:j + 1]
        scaled = work[j:j + 1] * (1.0 / pivot)
        pivots = jnp.where(rows == j, column, pivots)
        work = jnp.where(rows > j, work - column * scaled, work)
    return work[:, cols:] * lax.rsqrt(pivots[:, cols:])


def kernel(sizes, x_ref, kappa_ref, o_ref, first, second, parts, halves, packed, landed, gather_x, gather_y,
           face_send, face_recv, gx_send, gx_recv, gy_send, gy_recv):
    n_gx, n_gy, cols, nz, nx = sizes
    me_x, me_y = lax.axis_index("gx"), lax.axis_index("gy")
    groups = nz * nx
    lane = lax.broadcasted_iota(jnp.int32, (cols, LANES), 1)

    barrier = pltpu.get_barrier_semaphore()

    def at_x(index):
        return {"gx": index, "gy": me_y}

    def at_y(index):
        return {"gx": me_x, "gy": index}

    @pl.loop(1, n_gx)
    def _(k):
        pl.semaphore_signal(barrier, inc=1, device_id=at_x(lax.rem(me_x + k, n_gx)))

    @pl.loop(1, n_gy)
    def _(k):
        pl.semaphore_signal(barrier, inc=1, device_id=at_y(lax.rem(me_y + k, n_gy)))

    def pack(x, values, state):
        low, high = state
        for z in range(nz):
            g = z * nx + x
            rolled = pltpu.roll(values[z], g, 1)
            low = jnp.where(lane == g, rolled, low)
            high = jnp.where(lane == lax.rem(g + LANES - 1, LANES), rolled, high)
        return low, high

    def take(x, state):
        values = []
        for z in range(nz):
            value = x_ref[pl.ds(z * nx + x, cols, stride=groups), :]
            first[z, x + 1] = value
            values.append(value)
        return pack(x, values, state)

    def copies(field, phase):
        up_x = pltpu.make_async_remote_copy(
            src_ref=field.at[:, nx], dst_ref=field.at[:, 0], send_sem=face_send.at[phase, 0],
            recv_sem=face_recv.at[phase, 0], device_id=at_x(me_x + 1))
        down_x = pltpu.make_async_remote_copy(
            src_ref=field.at[:, 1], dst_ref=field.at[:, nx + 1], send_sem=face_send.at[phase, 1],
            recv_sem=face_recv.at[phase, 1], device_id=at_x(me_x - 1))
        up_y = pltpu.make_async_remote_copy(
            src_ref=packed.at[phase, 1], dst_ref=landed.at[phase, 0], send_sem=face_send.at[phase, 2],
            recv_sem=face_recv.at[phase, 2], device_id=at_y(me_y + 1))
        down_y = pltpu.make_async_remote_copy(
            src_ref=packed.at[phase, 0], dst_ref=landed.at[phase, 1], send_sem=face_send.at[phase, 3],
            recv_sem=face_recv.at[phase, 3], device_id=at_y(me_y - 1))
        return up_x, down_x, up_y, down_y

    def send(up, down, index, count):
        @pl.when(index < count - 1)
        def _():
            up.start()

        @pl.when(index > 0)
        def _():
            down.start()

    def receive(up, down, index, count):
        @pl.when(index > 0)
        def _():
            up.wait_recv()

        @pl.when(index < count - 1)
        def _():
            down.wait_recv()

    def finish(up, down, index, count):
        @pl.when(index < count - 1)
        def _():
            up.wait_send()

        @pl.when(index > 0)
        def _():
            down.wait_send()

    for field in (first, second):
        @pl.when(me_x == 0)
        def _():
            field[:, 0] = jnp.zeros((nz, cols, LANES), F32)

        @pl.when(me_x == n_gx - 1)
        def _():
            field[:, nx + 1] = jnp.zeros((nz, cols, LANES), F32)

    for phase in range(2):
        @pl.when(me_y == 0)
        def _():
            landed[phase, 0] = jnp.zeros((cols, LANES), F32)

        @pl.when(me_y == n_gy - 1)
        def _():
            landed[phase, 1] = jnp.zeros((cols, LANES), F32)

    zero = jnp.zeros((cols, LANES), F32)
    state = lax.fori_loop(0, 2, lambda i, s: take(i * (nx - 1), s), (zero, zero))
    pl.semaphore_wait(barrier, n_gx + n_gy - 2)
    up_x, down_x, up_y, down_y = copies(first, 0)
    send(up_x, down_x, me_x, n_gx)
    state = lax.fori_loop(1, nx - 1, take, state)
    packed[0, 0], packed[0, 1] = state
    send(up_y, down_y, me_y, n_gy)

    def apply_plane(field, phase, x):
        from_low, from_high = landed[phase, 0], landed[phase, 1]
        results = []
        for z in range(nz):
            g = z * nx + x
            center = field[z, x + 1]
            halo = jnp.where(lane == lax.rem(g + LANES - 1, LANES), from_low, from_high)
            halo = pltpu.roll(halo, lax.rem(LANES - g, LANES), 1)
            below = pltpu.roll(jnp.where(lane == LANES - 1, halo, center), 1, 1)
            above = pltpu.roll(jnp.where(lane == 0, halo, center), LANES - 1, 1)
            neighbours = field[z, x] + field[z, x + 2]
            neighbours = neighbours + (below + above)
            if z > 0:
                neighbours = neighbours + field[z - 1, x + 1]
            if z < nz - 1:
                neighbours = neighbours + field[z + 1, x + 1]
            coefficient = 6.0 + kappa_ref[pl.ds(g, 1), :]
            results.append(coefficient * center - neighbours)
        return results

    def first_plane(x, state):
        values = apply_plane(first, 0, x)
        for z in range(nz):
            second[z, x + 1] = values[z]
        return pack(x, values, state)

    receive(up_y, down_y, me_y, n_gy)
    state = lax.fori_loop(1, nx - 1, first_plane, (zero, zero))
    receive(up_x, down_x, me_x, n_gx)
    state = lax.fori_loop(0, 2, lambda i, s: first_plane(i * (nx - 1), s), state)
    packed[1, 0], packed[1, 1] = state
    finish(up_x, down_x, me_x, n_gx)
    finish(up_y, down_y, me_y, n_gy)
    up_x, down_x, up_y, down_y = copies(second, 1)
    send(up_y, down_y, me_y, n_gy)
    send(up_x, down_x, me_x, n_gx)

    def square(block):
        return lax.dot_general(block, block, (((1,), (1,)), ((), ())), preferred_element_type=F32)

    def second_plane(x, gram):
        values = apply_plane(second, 1, x)
        for pair in range(nz // 2):
            both = jnp.concatenate(values[2 * pair:2 * pair + 2], axis=1)
            block = jnp.concatenate(split(both, 3), axis=0)
            parts[x, pair] = block
            gram = gram + square(block)
        return gram

    receive(up_y, down_y, me_y, n_gy)
    gram = lax.fori_loop(1, nx - 1, second_plane, jnp.zeros((3 * cols, 3 * cols), F32))
    receive(up_x, down_x, me_x, n_gx)
    gram = lax.fori_loop(0, 2, lambda i, s: second_plane(i * (nx - 1), s), gram)
    finish(up_x, down_x, me_x, n_gx)
    finish(up_y, down_y, me_y, n_gy)

    def fold(gram, terms):
        rows = fold_rows(gram, cols, terms)
        total = rows[:, :cols]
        for i in range(1, terms):
            total = total + rows[:, i * cols:(i + 1) * cols]
        return total

    def exchange(slots, stage, value, axis_at, me, count, send_sem, recv_sem):
        slots[stage, me] = value

        def copy(k, slot):
            return pltpu.make_async_remote_copy(
                src_ref=slots.at[stage, slot], dst_ref=slots.at[stage, slot], send_sem=send_sem.at[stage, k],
                recv_sem=recv_sem.at[stage, slot], device_id=axis_at(lax.rem(me + k, count)))

        @pl.loop(1, count)
        def _(k):
            copy(k, me).start()

        @pl.loop(1, count)
        def _(k):
            copy(k, lax.rem(me + k, count)).wait_recv()

        total = slots[stage, 0]
        for i in range(1, count):
            total = total + slots[stage, i]

        @pl.loop(1, count)
        def _(k):
            copy(k, me).wait_send()

        return total

    def reduced(gram, stage):
        per = LANES // cols
        height = cols // per
        dense = jnp.concatenate([gram[i * height:(i + 1) * height] for i in range(per)], axis=1)
        dense = exchange(gather_x, stage, dense, at_x, me_x, n_gx, gx_send, gx_recv)
        dense = exchange(gather_y, stage, dense, at_y, me_y, n_gy, gy_send, gy_recv)
        return jnp.concatenate([dense[:, i * cols:(i + 1) * cols] for i in range(per)], axis=0)

    def stacked(matrix, terms):
        pieces = split(matrix, terms)
        return jnp.concatenate([jnp.concatenate([piece] * terms, axis=1) for piece in pieces], axis=0)

    inverse = stacked(inverse_factor(reduced(fold(gram, 3), 0), cols), 3)

    def solve_plane(x, gram):
        for pair in range(nz // 2):
            product = jnp.dot(inverse, parts[x, pair], preferred_element_type=F32)
            block = jnp.concatenate(split(fold_rows(product, cols, 3), 2), axis=0)
            halves[x, pair] = block
            gram = gram + square(block)
        return gram

    gram = lax.fori_loop(0, nx, solve_plane, jnp.zeros((2 * cols, 2 * cols), F32))
    scale = math.sqrt(n_gx * n_gy * groups * LANES)
    again = stacked(inverse_factor(reduced(fold(gram, 2), 1), cols) * scale, 2)

    @pl.loop(0, nx)
    def _(x):
        for pair in range(nz // 2):
            product = jnp.dot(again, halves[x, pair], preferred_element_type=F32)
            value = fold_rows(product, cols, 2)
            for side in range(2):
                g = (2 * pair + side) * nx + x
                o_ref[pl.ds(g, cols, stride=groups), :] = value[:, side * LANES:(side + 1) * LANES]


def solution(mesh):
    n_gx, n_gy = mesh.shape["gx"], mesh.shape["gy"]

    def body(test_block, kappa_sq):
        cols, nz, nx, ny = test_block.shape
        dma = pltpu.SemaphoreType.DMA
        vmem = pl.BlockSpec(memory_space=pltpu.VMEM)
        height = cols * cols // LANES
        result = pl.pallas_call(
            functools.partial(kernel, (n_gx, n_gy, cols, nz, nx)),
            out_shape=jax.ShapeDtypeStruct((cols * nz * nx, ny), F32),
            in_specs=[vmem, vmem],
            out_specs=vmem,
            scratch_shapes=[
                pltpu.VMEM((nz, nx + 2, cols, ny), F32),
                pltpu.VMEM((nz, nx + 2, cols, ny), F32),
                pltpu.VMEM((nx, nz // 2, 3 * cols, 2 * ny), BF16),
                pltpu.VMEM((nx, nz // 2, 2 * cols, 2 * ny), BF16),
                pltpu.VMEM((2, 2, cols, ny), F32),
                pltpu.VMEM((2, 2, cols, ny), F32),
                pltpu.VMEM((2, n_gx, height, LANES), F32),
                pltpu.VMEM((2, n_gy, height, LANES), F32),
                dma((2, 4)), dma((2, 4)),
                dma((2, n_gx)), dma((2, n_gx)),
                dma((2, n_gy)), dma((2, n_gy)),
            ],
            compiler_params=pltpu.CompilerParams(
                collective_id=0, has_side_effects=True, vmem_limit_bytes=48 * 1024 * 1024),
        )(test_block.reshape(cols * nz * nx, ny), kappa_sq.reshape(nz * nx, ny))
        return result.reshape(test_block.shape)

    in_specs = (P(None, None, "gx", "gy"), P(None, "gx", "gy"))
    out_specs = P(None, None, "gx", "gy")
    return jax.shard_map(body, mesh=mesh, in_specs=in_specs, out_specs=out_specs, check_vma=False)
```

time: 163 us -> 59.1 us (0.36)
  Pallas kernels: 0 us -> 55.2 us
  blocking collectives: 49.4 us -> 0 us
  other arithmetic: 47.9 us -> 0 us
  local copies, waits for them, and re-layouts: 31.8 us -> 3.75 us
  starting transfers between devices: 20.9 us -> 0 us
  matrix products: 11.5 us -> 0 us
    pallas_call x0 -> x1, Pallas kernels: none -> 55.2 us  [body(): pl.pallas_call(functools.partial(kernel, (n_gx, n_gy, cols, nz, nx)), out...]
    all_gather x4 -> x0, blocking collectives: 49.4 us -> none  [the longest x2 28.1 us: merged_factor(): lax.all_gather(column_factor[None], 'gy', axis=0, tiled=True)]
    ppermute x8 -> x0, starting transfers between devices: 20.9 us -> none  [the longest x4 15.5 us: extended(): lax.ppermute(lax.slice_in_dim(block, block.shape[dim] - width, None, axis...]
    another operation x16 -> x0, other arithmetic: 20.8 us -> none  [the longest x6 7.27 us: merged_factor(): column_factor = jnp.linalg.cholesky(jnp.sum(stacked, axis=0))]
    concatenate x2 -> x0, other arithmetic: 13 us -> none  [extended(): block = jnp.concatenate([low, block, high], axis=dim)]
    select_n x3 -> x0, other arithmetic: 10.4 us -> none  [the longest x1 9.07 us: body(): first_pass = jnp.where(inside_mask[None, None], first_pass, 0.0)]
    slice x6 -> x0, local copies, waits for them, and re-layouts: 8.45 us -> none  [the longest x2 4.01 us: stencil(): center = padded[:, :, 1:-1, 1:-1]]
    concatenate x2 -> x0, local copies, waits for them, and re-layouts: 8.4 us -> none  [extended(): block = jnp.concatenate([low, block, high], axis=dim)]
  transfers between devices with their start and end apart: 8 -> 0, of which waited for: 0 -> 0; matrix products, arithmetic and copies ran while one was open for 18% -> 0% of each run, Pallas kernels for 0% -> 0%
where the time goes in v1:
time: 59.1 us; the launch traced here: 58.9 us
  Pallas kernels  55.2 us (93%)
  local copies, waits for them, and re-layouts  3.75 us (6%)
    pallas_call x1, Pallas kernels, body(): pl.pallas_call(functools.partial(kernel, (n_gx, n_gy, cols, nz, nx)), out...  55.2 us
    unnamed x5, local copies, waits for them, and re-layouts  3.75 us

profile of v1, /device:TPU:0, one launch (start us, length us, event | category | flops | bytes accessed | tf_op | source)
XLA Modules:
  0.0 58.9 jit_solution(13805178781705405362)
XLA Ops:
  0.0 0.0 copy-start
  0.0 1.6 %copy-done = f32[32,8,16,128]{3,2,1,0:T(8,128)S(1)} copy-done((f32[32,8,16,128]{3,2,1,0:T(8,128)S(1)}, f32[32,8,16,128]{3,2,1,0:T(8,128)}, u32[]{:S(2)}) %copy-start) | copy-done | bytes 2097176
  1.6 0.0 copy-start.1
  1.6 0.8 %copy-done.1 = f32[8,16,128]{2,1,0:T(8,128)S(1)} copy-done((f32[8,16,128]{2,1,0:T(8,128)S(1)}, f32[8,16,128]{2,1,0:T(8,128)}, u32[]{:S(2)}) %copy-start.1) | copy-done | bytes 65560
  2.4 55.2 %shard_map.28 = f32[4096,128]{1,0:T(8,128)S(1)} custom-call(f32[4096,128]{1,0:T(8,128)S(1)} %bitcast.4, f32[128,128]{1,0:T(8,128)S(1)} %bitcast.5), custom_call_target="tpu_custom_call" | custom-call | tf_op jit(solution)/shard_map/pallas_call | solution.py:289
  57.6 1.3 %copy.4 = f32[32,8,16,128]{3,2,1,0:T(8,128)} copy(f32[32,8,16,128]{3,2,1,0:T(8,128)S(1)} %bitcast.3) | data formatting | bytes 4194304
Async XLA Ops:
  0.0 1.6 %copy-start = (f32[32,8,16,128]{3,2,1,0:T(8,128)S(1)}, f32[32,8,16,128]{3,2,1,0:T(8,128)}, u32[]{:S(2)}) copy-start(f32[32,8,16,128]{3,2,1,0:T(8,128)} %param.2) | copy-start | bytes 6291460
  1.6 0.8 %copy-start.1 = (f32[8,16,128]{2,1,0:T(8,128)S(1)}, f32[8,16,128]{2,1,0:T(8,128)}, u32[]{:S(2)}) copy-start(f32[8,16,128]{2,1,0:T(8,128)} %param.3) | copy-start | bytes 196612

commit v2 on v1

--- a/solution.py
+++ b/solution.py
@@ -44,13 +44,17 @@
     return work[:, cols:] * lax.rsqrt(pivots[:, cols:])
 
 
-def kernel(sizes, x_ref, kappa_ref, o_ref, first, second, parts, halves, packed, landed, gather_x, gather_y,
+def kernel(sizes, x_hbm, kappa_hbm, o_ref, x_ref, kappa_ref, load_sem, first, second, parts, halves, packed, landed, gather_x, gather_y,
            face_send, face_recv, gx_send, gx_recv, gy_send, gy_recv):
     n_gx, n_gy, cols, nz, nx = sizes
     me_x, me_y = lax.axis_index("gx"), lax.axis_index("gy")
     groups = nz * nx
     lane = lax.broadcasted_iota(jnp.int32, (cols, LANES), 1)
 
+    load_x = pltpu.make_async_copy(x_hbm, x_ref, load_sem.at[0])
+    load_kappa = pltpu.make_async_copy(kappa_hbm, kappa_ref, load_sem.at[1])
+    load_x.start()
+    load_kappa.start()
     barrier = pltpu.get_barrier_semaphore()
 
     def at_x(index):
@@ -91,13 +95,16 @@
         down_x = pltpu.make_async_remote_copy(
             src_ref=field.at[:, 1], dst_ref=field.at[:, nx + 1], send_sem=face_send.at[phase, 1],
             recv_sem=face_recv.at[phase, 1], device_id=at_x(me_x - 1))
+        return up_x, down_x
+
+    def copies_y(phase, half):
         up_y = pltpu.make_async_remote_copy(
-            src_ref=packed.at[phase, 1], dst_ref=landed.at[phase, 0], send_sem=face_send.at[phase, 2],
-            recv_sem=face_recv.at[phase, 2], device_id=at_y(me_y + 1))
+            src_ref=packed.at[phase, half, 1], dst_ref=landed.at[phase, half, 0], device_id=at_y(me_y + 1),
+            send_sem=face_send.at[phase, 2 + 2 * half], recv_sem=face_recv.at[phase, 2 + 2 * half])
         down_y = pltpu.make_async_remote_copy(
-            src_ref=packed.at[phase, 0], dst_ref=landed.at[phase, 1], send_sem=face_send.at[phase, 3],
-            recv_sem=face_recv.at[phase, 3], device_id=at_y(me_y - 1))
-        return up_x, down_x, up_y, down_y
+            src_ref=packed.at[phase, half, 0], dst_ref=landed.at[phase, half, 1], device_id=at_y(me_y - 1),
+            send_sem=face_send.at[phase, 3 + 2 * half], recv_sem=face_recv.at[phase, 3 + 2 * half])
+        return up_y, down_y
 
     def send(up, down, index, count):
         @pl.when(index < count - 1)
@@ -136,25 +143,37 @@
             field[:, nx + 1] = jnp.zeros((nz, cols, LANES), F32)
 
     for phase in range(2):
-        @pl.when(me_y == 0)
-        def _():
-            landed[phase, 0] = jnp.zeros((cols, LANES), F32)
-
-        @pl.when(me_y == n_gy - 1)
-        def _():
-            landed[phase, 1] = jnp.zeros((cols, LANES), F32)
+        for half in range(2):
+            @pl.when(me_y == 0)
+            def _():
+                landed[phase, half, 0] = jnp.zeros((cols, LANES), F32)
+
+            @pl.when(me_y == n_gy - 1)
+            def _():
+                landed[phase, half, 1] = jnp.zeros((cols, LANES), F32)
 
     zero = jnp.zeros((cols, LANES), F32)
-    state = lax.fori_loop(0, 2, lambda i, s: take(i * (nx - 1), s), (zero, zero))
+    middle = nx // 2
+    faces = [copies(first, 0), copies(second, 1)]
+    sides = [[copies_y(phase, half) for half in range(2)] for phase in range(2)]
+
+    def edges(step, state):
+        return lax.fori_loop(0, 2, lambda i, s: step(i * (nx - 1), s), state)
+
+    def send_side(phase, half, state):
+        packed[phase, half, 0], packed[phase, half, 1] = state
+        send(*sides[phase][half], me_y, n_gy)
+
+    load_x.wait()
+    state = edges(take, (zero, zero))
     pl.semaphore_wait(barrier, n_gx + n_gy - 2)
-    up_x, down_x, up_y, down_y = copies(first, 0)
-    send(up_x, down_x, me_x, n_gx)
-    state = lax.fori_loop(1, nx - 1, take, state)
-    packed[0, 0], packed[0, 1] = state
-    send(up_y, down_y, me_y, n_gy)
-
-    def apply_plane(field, phase, x):
-        from_low, from_high = landed[phase, 0], landed[phase, 1]
+    send(*faces[0], me_x, n_gx)
+    send_side(0, 0, lax.fori_loop(1, middle, take, (zero, zero)))
+    send_side(0, 1, lax.fori_loop(middle, nx - 1, take, state))
+    load_kappa.wait()
+
+    def apply_plane(field, phase, half, x):
+        from_low, from_high = landed[phase, half, 0], landed[phase, half, 1]
         results = []
         for z in range(nz):
             g = z * nx + x
@@ -173,41 +192,37 @@
             results.append(coefficient * center - neighbours)
         return results
 
-    def first_plane(x, state):
-        values = apply_plane(first, 0, x)
+    def first_plane(half, x, state):
+        values = apply_plane(first, 0, half, x)
         for z in range(nz):
             second[z, x + 1] = values[z]
         return pack(x, values, state)
 
-    receive(up_y, down_y, me_y, n_gy)
-    state = lax.fori_loop(1, nx - 1, first_plane, (zero, zero))
-    receive(up_x, down_x, me_x, n_gx)
-    state = lax.fori_loop(0, 2, lambda i, s: first_plane(i * (nx - 1), s), state)
-    packed[1, 0], packed[1, 1] = state
-    finish(up_x, down_x, me_x, n_gx)
-    finish(up_y, down_y, me_y, n_gy)
-    up_x, down_x, up_y, down_y = copies(second, 1)
-    send(up_y, down_y, me_y, n_gy)
-    send(up_x, down_x, me_x, n_gx)
+    receive(*sides[0][0], me_y, n_gy)
+    state = lax.fori_loop(1, middle, functools.partial(first_plane, 0), (zero, zero))
+    send_side(1, 0, state)
+    receive(*sides[0][1], me_y, n_gy)
+    receive(*faces[0], me_x, n_gx)
+    state = edges(functools.partial(first_plane, 1), (zero, zero))
+    send(*faces[1], me_x, n_gx)
+    send_side(1, 1, lax.fori_loop(middle, nx - 1, functools.partial(first_plane, 1), state))
 
     def square(block):
         return lax.dot_general(block, block, (((1,), (1,)), ((), ())), preferred_element_type=F32)
 
-    def second_plane(x, gram):
-        values = apply_plane(second, 1, x)
-        for pair in range(nz // 2):
-            both = jnp.concatenate(values[2 * pair:2 * pair + 2], axis=1)
-            block = jnp.concatenate(split(both, 3), axis=0)
-            parts[x, pair] = block
-            gram = gram + square(block)
-        return gram
-
-    receive(up_y, down_y, me_y, n_gy)
-    gram = lax.fori_loop(1, nx - 1, second_plane, jnp.zeros((3 * cols, 3 * cols), F32))
-    receive(up_x, down_x, me_x, n_gx)
-    gram = lax.fori_loop(0, 2, lambda i, s: second_plane(i * (nx - 1), s), gram)
-    finish(up_x, down_x, me_x, n_gx)
-    finish(up_y, down_y, me_y, n_gy)
+    def second_plane(half, x, gram):
+        values = jnp.concatenate(apply_plane(second, 1, half, x), axis=1)
+        block = jnp.concatenate(split(values, 3), axis=0)
+        parts[x] = block
+        return gram + square(block)
+
+    receive(*sides[1][0], me_y, n_gy)
+    gram = jnp.zeros((3 * cols, 3 * cols), F32)
+    gram = lax.fori_loop(1, middle, functools.partial(second_plane, 0), gram)
+    receive(*sides[1][1], me_y, n_gy)
+    gram = lax.fori_loop(middle, nx - 1, functools.partial(second_plane, 1), gram)
+    receive(*faces[1], me_x, n_gx)
+    gram = edges(functools.partial(second_plane, 1), gram)
 
     def fold(gram, terms):
         rows = fold_rows(gram, cols, terms)
@@ -216,13 +231,16 @@
             total = total + rows[:, i * cols:(i + 1) * cols]
         return total
 
+    def gather_copy(slots, stage, k, slot, axis_at, me, count, send_sem, recv_sem):
+        return pltpu.make_async_remote_copy(
+            src_ref=slots.at[stage, slot], dst_ref=slots.at[stage, slot], send_sem=send_sem.at[stage, k],
+            recv_sem=recv_sem.at[stage, slot], device_id=axis_at(lax.rem(me + k, count)))
+
     def exchange(slots, stage, value, axis_at, me, count, send_sem, recv_sem):
         slots[stage, me] = value
 
         def copy(k, slot):
-            return pltpu.make_async_remote_copy(
-                src_ref=slots.at[stage, slot], dst_ref=slots.at[stage, slot], send_sem=send_sem.at[stage, k],
-                recv_sem=recv_sem.at[stage, slot], device_id=axis_at(lax.rem(me + k, count)))
+            return gather_copy(slots, stage, k, slot, axis_at, me, count, send_sem, recv_sem)
 
         @pl.loop(1, count)
         def _(k):
@@ -235,10 +253,6 @@
         total = slots[stage, 0]
         for i in range(1, count):
             total = total + slots[stage, i]
-
-        @pl.loop(1, count)
-        def _(k):
-            copy(k, me).wait_send()
 
         return total
 
@@ -250,32 +264,42 @@
         dense = exchange(gather_y, stage, dense, at_y, me_y, n_gy, gy_send, gy_recv)
         return jnp.concatenate([dense[:, i * cols:(i + 1) * cols] for i in range(per)], axis=0)
 
-    def stacked(matrix, terms):
+    def rows(stack, order):
+        return jnp.concatenate([stack[i * cols:(i + 1) * cols] for i in order], axis=0)
+
+    def columns(matrix, terms, order):
         pieces = split(matrix, terms)
-        return jnp.concatenate([jnp.concatenate([piece] * terms, axis=1) for piece in pieces], axis=0)
-
-    inverse = stacked(inverse_factor(reduced(fold(gram, 3), 0), cols), 3)
+        return jnp.concatenate([pieces[i] for i in order], axis=1)
+
+    inverse = columns(inverse_factor(reduced(fold(gram, 3), 0), cols), 3, (0, 0, 0, 1, 1, 2))
 
     def solve_plane(x, gram):
-        for pair in range(nz // 2):
-            product = jnp.dot(inverse, parts[x, pair], preferred_element_type=F32)
-            block = jnp.concatenate(split(fold_rows(product, cols, 3), 2), axis=0)
-            halves[x, pair] = block
-            gram = gram + square(block)
-        return gram
-
-    gram = lax.fori_loop(0, nx, solve_plane, jnp.zeros((2 * cols, 2 * cols), F32))
+        product = jnp.dot(inverse, rows(parts[x], (0, 1, 2, 0, 1, 0)), preferred_element_type=F32)
+        block = jnp.concatenate(split(product, 2), axis=0)
+        halves[x] = block
+        return gram + square(block)
+
+    gram = lax.fori_loop(0, nx, solve_plane, jnp.zeros((2 * cols, 2 * cols), F32), unroll=2)
     scale = math.sqrt(n_gx * n_gy * groups * LANES)
-    again = stacked(inverse_factor(reduced(fold(gram, 2), 1), cols) * scale, 2)
-
-    @pl.loop(0, nx)
-    def _(x):
-        for pair in range(nz // 2):
-            product = jnp.dot(again, halves[x, pair], preferred_element_type=F32)
-            value = fold_rows(product, cols, 2)
-            for side in range(2):
-                g = (2 * pair + side) * nx + x
-                o_ref[pl.ds(g, cols, stride=groups), :] = value[:, side * LANES:(side + 1) * LANES]
+    again = columns(inverse_factor(reduced(fold(gram, 2), 1), cols) * scale, 2, (0, 0, 1, 1))
+
+    def finish_plane(x, carry):
+        value = jnp.dot(again, rows(halves[x], (0, 1, 0, 1)), preferred_element_type=F32)
+        for z in range(nz):
+            o_ref[pl.ds(z * nx + x, cols, stride=groups), :] = value[:, z * LANES:(z + 1) * LANES]
+        return carry
+
+    lax.fori_loop(0, nx, finish_plane, 0, unroll=2)
+
+    for phase in range(2):
+        finish(*faces[phase], me_x, n_gx)
+        for half in range(2):
+            finish(*sides[phase][half], me_y, n_gy)
+        for slots, axis_at, me, count, send_sem, recv_sem in (
+                (gather_x, at_x, me_x, n_gx, gx_send, gx_recv), (gather_y, at_y, me_y, n_gy, gy_send, gy_recv)):
+            @pl.loop(1, count)
+            def _(k):
+                gather_copy(slots, phase, k, me, axis_at, me, count, send_sem, recv_sem).wait_send()
 
 
 def solution(mesh):
@@ -289,18 +313,21 @@
         result = pl.pallas_call(
             functools.partial(kernel, (n_gx, n_gy, cols, nz, nx)),
             out_shape=jax.ShapeDtypeStruct((cols * nz * nx, ny), F32),
-            in_specs=[vmem, vmem],
+            in_specs=[pl.BlockSpec(memory_space=pl.ANY)] * 2,
             out_specs=vmem,
             scratch_shapes=[
+                pltpu.VMEM((cols * nz * nx, ny), F32),
+                pltpu.VMEM((nz * nx, ny), F32),
+                dma((2,)),
                 pltpu.VMEM((nz, nx + 2, cols, ny), F32),
                 pltpu.VMEM((nz, nx + 2, cols, ny), F32),
-                pltpu.VMEM((nx, nz // 2, 3 * cols, 2 * ny), BF16),
-                pltpu.VMEM((nx, nz // 2, 2 * cols, 2 * ny), BF16),
-                pltpu.VMEM((2, 2, cols, ny), F32),
-                pltpu.VMEM((2, 2, cols, ny), F32),
+                pltpu.VMEM((nx, 3 * cols, nz * ny), BF16),
+                pltpu.VMEM((nx, 2 * cols, nz * ny), BF16),
+                pltpu.VMEM((2, 2, 2, cols, ny), F32),
+                pltpu.VMEM((2, 2, 2, cols, ny), F32),
                 pltpu.VMEM((2, n_gx, height, LANES), F32),
                 pltpu.VMEM((2, n_gy, height, LANES), F32),
-                dma((2, 4)), dma((2, 4)),
+                dma((2, 6)), dma((2, 6)),
                 dma((2, n_gx)), dma((2, n_gx)),
                 dma((2, n_gy)), dma((2, n_gy)),
             ],

time: 59.1 us -> 51.4 us (0.87)
  Pallas kernels: 55.2 us -> 47.5 us
    pallas_call x1, Pallas kernels: 55.2 us -> 47.5 us  [body(): pl.pallas_call(functools.partial(kernel, (n_gx, n_gy, cols, nz, nx)), out...]
where the time goes in v2:
time: 51.4 us; the launch traced here: 51.2 us
  Pallas kernels  47.5 us (92%)
  local copies, waits for them, and re-layouts  3.75 us (7%)
    pallas_call x1, Pallas kernels, body(): pl.pallas_call(functools.partial(kernel, (n_gx, n_gy, cols, nz, nx)), out...  47.5 us
    unnamed x5, local copies, waits for them, and re-layouts  3.75 us

profile of v2, /device:TPU:0, one launch (start us, length us, event | category | flops | bytes accessed | tf_op | source)
XLA Modules:
  0.0 51.2 jit_solution(629310076227065079)
XLA Ops:
  0.0 0.0 copy-start
  0.0 1.6 %copy-done = f32[32,8,16,128]{3,2,1,0:T(8,128)S(1)} copy-done((f32[32,8,16,128]{3,2,1,0:T(8,128)S(1)}, f32[32,8,16,128]{3,2,1,0:T(8,128)}, u32[]{:S(2)}) %copy-start) | copy-done | bytes 2097176
  1.6 0.0 copy-start.1
  1.6 0.8 %copy-done.1 = f32[8,16,128]{2,1,0:T(8,128)S(1)} copy-done((f32[8,16,128]{2,1,0:T(8,128)S(1)}, f32[8,16,128]{2,1,0:T(8,128)}, u32[]{:S(2)}) %copy-start.1) | copy-done | bytes 65560
  2.4 47.5 %shard_map.28 = f32[4096,128]{1,0:T(8,128)S(1)} custom-call(f32[4096,128]{1,0:T(8,128)S(1)} %bitcast.4, f32[128,128]{1,0:T(8,128)S(1)} %bitcast.5), custom_call_target="tpu_custom_call" | custom-call | tf_op jit(solution)/shard_map/pallas_call | solution.py:313
  49.9 1.3 %copy.4 = f32[32,8,16,128]{3,2,1,0:T(8,128)} copy(f32[32,8,16,128]{3,2,1,0:T(8,128)S(1)} %bitcast.3) | data formatting | bytes 4194304
Async XLA Ops:
  0.0 1.6 %copy-start = (f32[32,8,16,128]{3,2,1,0:T(8,128)S(1)}, f32[32,8,16,128]{3,2,1,0:T(8,128)}, u32[]{:S(2)}) copy-start(f32[32,8,16,128]{3,2,1,0:T(8,128)} %param.2) | copy-start | bytes 6291460
  1.6 0.8 %copy-start.1 = (f32[8,16,128]{2,1,0:T(8,128)S(1)}, f32[8,16,128]{2,1,0:T(8,128)}, u32[]{:S(2)}) copy-start(f32[8,16,128]{2,1,0:T(8,128)} %param.3) | copy-start | bytes 196612

commit v3 on v2

--- a/solution.py
+++ b/solution.py
@@ -218,9 +218,9 @@
 
     receive(*sides[1][0], me_y, n_gy)
     gram = jnp.zeros((3 * cols, 3 * cols), F32)
-    gram = lax.fori_loop(1, middle, functools.partial(second_plane, 0), gram)
+    gram = lax.fori_loop(1, middle, functools.partial(second_plane, 0), gram, unroll=True)
     receive(*sides[1][1], me_y, n_gy)
-    gram = lax.fori_loop(middle, nx - 1, functools.partial(second_plane, 1), gram)
+    gram = lax.fori_loop(middle, nx - 1, functools.partial(second_plane, 1), gram, unroll=True)
     receive(*faces[1], me_x, n_gx)
     gram = edges(functools.partial(second_plane, 1), gram)
 
@@ -279,7 +279,7 @@
         halves[x] = block
         return gram + square(block)
 
-    gram = lax.fori_loop(0, nx, solve_plane, jnp.zeros((2 * cols, 2 * cols), F32), unroll=2)
+    gram = lax.fori_loop(0, nx, solve_plane, jnp.zeros((2 * cols, 2 * cols), F32), unroll=4)
     scale = math.sqrt(n_gx * n_gy * groups * LANES)
     again = columns(inverse_factor(reduced(fold(gram, 2), 1), cols) * scale, 2, (0, 0, 1, 1))
 
@@ -289,7 +289,7 @@
             o_ref[pl.ds(z * nx + x, cols, stride=groups), :] = value[:, z * LANES:(z + 1) * LANES]
         return carry
 
-    lax.fori_loop(0, nx, finish_plane, 0, unroll=2)
+    lax.fori_loop(0, nx, finish_plane, 0, unroll=4)
 
     for phase in range(2):
         finish(*faces[phase], me_x, n_gx)
@@ -313,7 +313,7 @@
         result = pl.pallas_call(
             functools.partial(kernel, (n_gx, n_gy, cols, nz, nx)),
             out_shape=jax.ShapeDtypeStruct((cols * nz * nx, ny), F32),
-            in_specs=[pl.BlockSpec(memory_space=pl.ANY)] * 2,
+            in_specs=[pl.BlockSpec(memory_space=pltpu.HBM)] * 2,
             out_specs=vmem,
             scratch_shapes=[
                 pltpu.VMEM((cols * nz * nx, ny), F32),

time: 51.4 us -> 48.6 us (0.946)
  Pallas kernels: 47.5 us -> 44.7 us
    pallas_call x1, Pallas kernels: 47.5 us -> 44.7 us  [body(): pl.pallas_call(functools.partial(kernel, (n_gx, n_gy, cols, nz, nx)), out...]
where the time goes in v3:
time: 48.6 us; the launch traced here: 48.5 us
  Pallas kernels  44.7 us (92%)
  local copies, waits for them, and re-layouts  3.75 us (8%)
    pallas_call x1, Pallas kernels, body(): pl.pallas_call(functools.partial(kernel, (n_gx, n_gy, cols, nz, nx)), out...  44.7 us
    unnamed x5, local copies, waits for them, and re-layouts  3.75 us

profile of v3, /device:TPU:0, one launch (start us, length us, event | category | flops | bytes accessed | tf_op | source)
XLA Modules:
  0.0 48.5 jit_solution(2740215974073519662)
XLA Ops:
  0.0 0.0 copy-start
  0.0 1.6 %copy-done = f32[32,8,16,128]{3,2,1,0:T(8,128)S(1)} copy-done((f32[32,8,16,128]{3,2,1,0:T(8,128)S(1)}, f32[32,8,16,128]{3,2,1,0:T(8,128)}, u32[]{:S(2)}) %copy-start) | copy-done | bytes 2097176
  1.6 0.0 copy-start.1
  1.6 0.8 %copy-done.1 = f32[8,16,128]{2,1,0:T(8,128)S(1)} copy-done((f32[8,16,128]{2,1,0:T(8,128)S(1)}, f32[8,16,128]{2,1,0:T(8,128)}, u32[]{:S(2)}) %copy-start.1) | copy-done | bytes 65560
  2.4 44.7 %shard_map.28 = f32[4096,128]{1,0:T(8,128)S(1)} custom-call(f32[4096,128]{1,0:T(8,128)S(1)} %bitcast.4, f32[128,128]{1,0:T(8,128)S(1)} %bitcast.5), custom_call_target="tpu_custom_call" | custom-call | tf_op jit(solution)/shard_map/pallas_call | solution.py:313
  47.1 1.3 %copy.4 = f32[32,8,16,128]{3,2,1,0:T(8,128)} copy(f32[32,8,16,128]{3,2,1,0:T(8,128)S(1)} %bitcast.3) | data formatting | bytes 4194304
Async XLA Ops:
  0.0 1.6 %copy-start = (f32[32,8,16,128]{3,2,1,0:T(8,128)S(1)}, f32[32,8,16,128]{3,2,1,0:T(8,128)}, u32[]{:S(2)}) copy-start(f32[32,8,16,128]{3,2,1,0:T(8,128)} %param.2) | copy-start | bytes 6291460
  1.6 0.8 %copy-start.1 = (f32[8,16,128]{2,1,0:T(8,128)S(1)}, f32[8,16,128]{2,1,0:T(8,128)}, u32[]{:S(2)}) copy-start(f32[8,16,128]{2,1,0:T(8,128)} %param.3) | copy-start | bytes 196612

commit v4 on v3

--- a/solution.py
+++ b/solution.py
@@ -44,7 +44,7 @@
     return work[:, cols:] * lax.rsqrt(pivots[:, cols:])
 
 
-def kernel(sizes, x_hbm, kappa_hbm, o_ref, x_ref, kappa_ref, load_sem, first, second, parts, halves, packed, landed, gather_x, gather_y,
+def kernel(sizes, x_hbm, kappa_hbm, halves_hbm, again_ref, x_ref, kappa_ref, load_sem, store_sem, first, second, parts, halves, packed, landed, gather_x, gather_y,
            face_send, face_recv, gx_send, gx_recv, gy_send, gy_recv):
     n_gx, n_gy, cols, nz, nx = sizes
     me_x, me_y = lax.axis_index("gx"), lax.axis_index("gy")
@@ -277,19 +277,16 @@
         product = jnp.dot(inverse, rows(parts[x], (0, 1, 2, 0, 1, 0)), preferred_element_type=F32)
         block = jnp.concatenate(split(product, 2), axis=0)
         halves[x] = block
+        pltpu.make_async_copy(halves.at[x], halves_hbm.at[x], store_sem.at[x]).start()
         return gram + square(block)
 
     gram = lax.fori_loop(0, nx, solve_plane, jnp.zeros((2 * cols, 2 * cols), F32), unroll=4)
     scale = math.sqrt(n_gx * n_gy * groups * LANES)
-    again = columns(inverse_factor(reduced(fold(gram, 2), 1), cols) * scale, 2, (0, 0, 1, 1))
-
-    def finish_plane(x, carry):
-        value = jnp.dot(again, rows(halves[x], (0, 1, 0, 1)), preferred_element_type=F32)
-        for z in range(nz):
-            o_ref[pl.ds(z * nx + x, cols, stride=groups), :] = value[:, z * LANES:(z + 1) * LANES]
-        return carry
-
-    lax.fori_loop(0, nx, finish_plane, 0, unroll=4)
+    again_ref[...] = columns(inverse_factor(reduced(fold(gram, 2), 1), cols) * scale, 2, (0, 0, 1, 1))
+
+    @pl.loop(0, nx)
+    def _(x):
+        pltpu.make_async_copy(halves.at[x], halves_hbm.at[x], store_sem.at[x]).wait()
 
     for phase in range(2):
         finish(*faces[phase], me_x, n_gx)
@@ -302,6 +299,20 @@
                 gather_copy(slots, phase, k, me, axis_at, me, count, send_sem, recv_sem).wait_send()
 
 
+def finish_kernel(again_ref, halves_ref, o_ref):
+    cols, deep, nx, ny = o_ref.shape
+    flat = o_ref.reshape(cols * deep * nx, ny)
+
+    def plane(x, carry):
+        block = halves_ref[x]
+        value = jnp.dot(again_ref[...], jnp.concatenate([block, block], axis=0), preferred_element_type=F32)
+        for z in range(deep):
+            flat[pl.ds(z * nx + x, cols, stride=deep * nx), :] = value[:, z * ny:(z + 1) * ny]
+        return carry
+
+    lax.fori_loop(0, nx, plane, 0, unroll=4)
+
+
 def solution(mesh):
     n_gx, n_gy = mesh.shape["gx"], mesh.shape["gy"]
 
@@ -310,15 +321,16 @@
         dma = pltpu.SemaphoreType.DMA
         vmem = pl.BlockSpec(memory_space=pltpu.VMEM)
         height = cols * cols // LANES
-        result = pl.pallas_call(
+        halves, again = pl.pallas_call(
             functools.partial(kernel, (n_gx, n_gy, cols, nz, nx)),
-            out_shape=jax.ShapeDtypeStruct((cols * nz * nx, ny), F32),
+            out_shape=(jax.ShapeDtypeStruct((nx, 2 * cols, nz * ny), BF16),
+                       jax.ShapeDtypeStruct((cols, 4 * cols), BF16)),
             in_specs=[pl.BlockSpec(memory_space=pltpu.HBM)] * 2,
-            out_specs=vmem,
+            out_specs=(pl.BlockSpec(memory_space=pltpu.HBM), vmem),
             scratch_shapes=[
                 pltpu.VMEM((cols * nz * nx, ny), F32),
                 pltpu.VMEM((nz * nx, ny), F32),
-                dma((2,)),
+                dma((2,)), dma((nx,)),
                 pltpu.VMEM((nz, nx + 2, cols, ny), F32),
                 pltpu.VMEM((nz, nx + 2, cols, ny), F32),
                 pltpu.VMEM((nx, 3 * cols, nz * ny), BF16),
@@ -332,9 +344,17 @@
                 dma((2, n_gy)), dma((2, n_gy)),
             ],
             compiler_params=pltpu.CompilerParams(
-                collective_id=0, has_side_effects=True, vmem_limit_bytes=48 * 1024 * 1024),
+                collective_id=0, has_side_effects=True, vmem_limit_bytes=62 * 1024 * 1024),
         )(test_block.reshape(cols * nz * nx, ny), kappa_sq.reshape(nz * nx, ny))
-        return result.reshape(test_block.shape)
+        wide = 8
+        return pl.pallas_call(
+            finish_kernel,
+            out_shape=jax.ShapeDtypeStruct(test_block.shape, F32),
+            grid=(nx // wide,),
+            in_specs=[vmem, pl.BlockSpec((wide, 2 * cols, nz * ny), lambda i: (i, 0, 0))],
+            out_specs=pl.BlockSpec((cols, nz, wide, ny), lambda i: (0, 0, i, 0)),
+            compiler_params=pltpu.CompilerParams(vmem_limit_bytes=62 * 1024 * 1024),
+        )(again, halves)
 
     in_specs = (P(None, None, "gx", "gy"), P(None, "gx", "gy"))
     out_specs = P(None, None, "gx", "gy")

time: 48.6 us -> 47.1 us (0.969)
  local copies, waits for them, and re-layouts: 3.75 us -> 0 us
  Pallas kernels: 44.7 us -> 46.9 us
    pallas_call x0 -> x1, Pallas kernels: none -> 4.13 us  [body(): pl.pallas_call(finish_kernel, out_shape=jax.ShapeDtypeStruct(test_block.s...]
    unnamed x5 -> x0, local copies, waits for them, and re-layouts: 3.75 us -> none
    pallas_call x1, Pallas kernels: 44.7 us -> 42.8 us  [body(): pl.pallas_call(functools.partial(kernel, (n_gx, n_gy, cols, nz, nx)), out...]
where the time goes in v4:
time: 47.1 us; the launch traced here: 46.9 us
  Pallas kernels  46.9 us (100%)
    pallas_call x1, Pallas kernels, body(): pl.pallas_call(functools.partial(kernel, (n_gx, n_gy, cols, nz, nx)), out...  42.8 us
    pallas_call x1, Pallas kernels, body(): pl.pallas_call(finish_kernel, out_shape=jax.ShapeDtypeStruct(test_block.s...  4.13 us

profile of v4, /device:TPU:0, one launch (start us, length us, event | category | flops | bytes accessed | tf_op | source)
XLA Modules:
  0.0 46.9 jit_solution(15428203691080789609)
XLA Ops:
  0.0 42.8 %shard_map.28 = (bf16[16,64,1024]{2,1,0:T(8,128)(2,1)}, bf16[32,128]{1,0:T(8,128)(2,1)}) custom-call(f32[4096,128]{1,0:T(8,128)} %bitcast.2, f32[128,128]{1,0:T(8,128)} %bitcast.3), custom_call_target="tpu_custom_call" | custom-call | tf_op jit(solution)/shard_map/pallas_call | solution.py:324
  42.8 4.1 %shard_map.29 = f32[32,8,16,128]{3,2,1,0:T(8,128)} custom-call(bf16[32,128]{1,0:T(8,128)(2,1)} %get-tuple-element.7.again_ref, bf16[16,64,1024]{2,1,0:T(8,128)(2,1)} %get-tuple-element.8.halves_ref), custom_call_target="tpu_custom_call" | custom-call | tf_op jit(solution)/shard_map/pallas_call | solution.py:350

commit v5 on v4

--- a/solution.py
+++ b/solution.py
@@ -310,7 +310,7 @@
             flat[pl.ds(z * nx + x, cols, stride=deep * nx), :] = value[:, z * ny:(z + 1) * ny]
         return carry
 
-    lax.fori_loop(0, nx, plane, 0, unroll=4)
+    lax.fori_loop(0, nx, plane, 0, unroll=8)
 
 
 def solution(mesh):

time: 47.1 us -> 46.8 us (level)
  no operation moved by 1% of the time
where the time goes in v5:
time: 46.8 us; the launch traced here: 46.7 us
  Pallas kernels  46.7 us (100%)
    pallas_call x1, Pallas kernels, body(): pl.pallas_call(functools.partial(kernel, (n_gx, n_gy, cols, nz, nx)), out...  42.8 us
    pallas_call x1, Pallas kernels, body(): pl.pallas_call(finish_kernel, out_shape=jax.ShapeDtypeStruct(test_block.s...  3.9 us

profile of v5, /device:TPU:0, one launch (start us, length us, event | category | flops | bytes accessed | tf_op | source)
XLA Modules:
  0.0 46.7 jit_solution(17457127011638933518)
XLA Ops:
  0.0 42.8 %shard_map.28 = (bf16[16,64,1024]{2,1,0:T(8,128)(2,1)}, bf16[32,128]{1,0:T(8,128)(2,1)}) custom-call(f32[4096,128]{1,0:T(8,128)} %bitcast.2, f32[128,128]{1,0:T(8,128)} %bitcast.3), custom_call_target="tpu_custom_call" | custom-call | tf_op jit(solution)/shard_map/pallas_call | solution.py:324
  42.8 3.9 %shard_map.29 = f32[32,8,16,128]{3,2,1,0:T(8,128)} custom-call(bf16[32,128]{1,0:T(8,128)(2,1)} %get-tuple-element.7.again_ref, bf16[16,64,1024]{2,1,0:T(8,128)(2,1)} %get-tuple-element.8.halves_ref), custom_call_target="tpu_custom_call" | custom-call | tf_op jit(solution)/shard_map/pallas_call | solution.py:350
